TPU v7x, 256 devices: a whole 4x4x8 slice. The times are simulated.
256 devices in a mesh: span: 64 (over y_lo, x, z), tile: 4 (over y_hi, core).
Axes of the slice: x: 4, y: 4 (y_hi: 2, y_lo: 2; y = y_hi * 2 + y_lo), z: 8, core: 2. Of those that a mesh axis runs over, the one named last changes fastest.
Arguments:
- features: bfloat16 [64, 41, 16, 768], P('span', None, 'tile'), may hold values from -10 to 10
- clip_lengths: int32 [64], replicated, may hold values from 1 to 41, as said below
- slot_table: int32 [64, 41], replicated, may hold values from -1 to 2047, as said below
- gain_one: float32 [384], replicated, may hold values from 0.25 to 1.75
- weight_one: bfloat16 [3, 3, 3, 384, 384], replicated, may hold values from -0.0625 to 0.0625
- gain_two: float32 [384], replicated, may hold values from 0.25 to 1.75
- weight_two: bfloat16 [3, 3, 3, 384, 384], replicated, may hold values from -0.0625 to 0.0625
Outputs:
- decoded: bfloat16 [2048, 16, 768], P('span', 'tile')
Inputs may be any that keep to these rules, and one draw needn't show every extreme that they name: `clip_lengths`: the lengths add up to 32 times the number of tenants, and one clip has exactly 41 frames. `slot_table`: entries with f < clip_lengths[t] name every work slot exactly once, so that work slots d * 32 to d * 32 + 32 - 1 (those of index d of span) hold exactly 32 frames; at most 1 frames of one clip fall into the slots of one index of span, and in every draw some clip puts exactly 1 there. Entries with f >= clip_lengths[t] are -1.
All inputs are finite; a program needn't handle non-finite values.
Results may differ from a plain program's by a relative error of at most 0.0038.
Values may be sent and summed in bfloat16 or wider, within the bound.
A program may use at most 128 MiB of HBM per device.

v0:
```python
import jax
import jax.numpy as jnp
from jax import lax
from jax.sharding import PartitionSpec as P

WSLOT = 32


def with_halo(cells, sides, width):
    for axis, dim in sides:
        count = lax.axis_size(axis)
        ends = count - 1
        head = lax.slice_in_dim(cells, 0, width, axis=dim)
        tail = lax.slice_in_dim(cells, cells.shape[dim] - width, cells.shape[dim], axis=dim)
        cells = jnp.concatenate(
            [
                lax.ppermute(tail, axis, [(i, (i + 1) % count) for i in range(ends)]),
                cells,
                lax.ppermute(head, axis, [((i + 1) % count, i) for i in range(ends)]),
            ],
            axis=dim,
        )
    return cells


def activate(values, gain_vec):
    channels = gain_vec.shape[0]
    widened = values.astype(jnp.float32)
    shaped = widened.reshape(widened.shape[:-1] + (widened.shape[-1] // channels, channels))
    scaled = (
        shaped * lax.rsqrt(jnp.mean(shaped * shaped, axis=-1, keepdims=True) + 1e-06) * gain_vec
    )
    return jax.nn.silu(scaled).astype(jnp.bfloat16).reshape(values.shape)


def causal_conv(padded, weight):
    channels = weight.shape[-1]
    stacks, frame_count, row_count, breadth = padded.shape
    columns = breadth // channels
    shaped = padded.reshape(stacks, frame_count, row_count, columns, channels)
    shaped = jnp.pad(shaped, ((0, 0), (0, 0), (0, 0), (1, 1), (0, 0)))
    out_frames = frame_count - 2
    out_rows = row_count - 2
    summed = jnp.zeros((stacks, out_frames, out_rows, columns, channels), jnp.float32)
    for time_tap in range(3):
        for row_tap in range(3):
            for column_tap in range(3):
                window = shaped[
                    :,
                    time_tap : time_tap + out_frames,
                    row_tap : row_tap + out_rows,
                    column_tap : column_tap + columns,
                ]
                summed = summed + jnp.einsum(
                    "bfrwc,cd->bfrwd",
                    window,
                    weight[time_tap, row_tap, column_tap],
                    preferred_element_type=jnp.float32,
                )
    return summed.reshape(stacks, out_frames, out_rows, breadth)


def residual_block(frames_in, gain_one, weight_one, gain_two, weight_two):
    act_one = with_halo(activate(frames_in, gain_one), (("tile", 2),), 1)
    hidden = causal_conv(act_one, weight_one).astype(jnp.bfloat16)
    act_two = with_halo(activate(hidden, gain_two), (("tile", 2),), 1)
    branch = causal_conv(act_two, weight_two)
    return (frames_in[:, 4:].astype(jnp.float32) + branch).astype(jnp.bfloat16)


def local(features, clip_lengths, slot_table, gain_one, weight_one, gain_two, weight_two):
    groups = lax.axis_size("span")
    position = lax.axis_index("span")
    frame_count = features.shape[1]
    capacity = (frame_count + groups - 1) // groups
    frame_ids = jnp.arange(frame_count, dtype=jnp.int32)
    alive_mask = frame_ids[None, :] < clip_lengths[:, None]
    target = jnp.where(alive_mask, slot_table // WSLOT, -1)
    before = frame_ids[:, None] > frame_ids[None, :]
    same_dest = (target[:, :, None] == target[:, None, :]) & alive_mask[:, None, :] & before[None]
    rank_table = jnp.sum(same_dest.astype(jnp.int32), axis=2)
    own_target = lax.dynamic_index_in_dim(target, position, 0, keepdims=False)
    own_rank = lax.dynamic_index_in_dim(rank_table, position, 0, keepdims=False)
    dest_ids = jnp.arange(groups, dtype=jnp.int32)
    cap_ids = jnp.arange(capacity, dtype=jnp.int32)
    outgoing = (
        (own_target[None, None, :] == dest_ids[:, None, None])
        & (own_rank[None, None, :] == cap_ids[None, :, None])
    ).astype(jnp.bfloat16)
    slot_ids = position * WSLOT + jnp.arange(WSLOT, dtype=jnp.int32)
    matched = (slot_table[None, :, :] == slot_ids[:, None, None]) & alive_mask[None]
    incoming = jnp.sum(
        (matched[..., None] & (rank_table[None, :, :, None] == cap_ids)).astype(jnp.float32), axis=2
    ).astype(jnp.bfloat16)
    clip_frames = features[0]
    padded = jnp.concatenate(
        [jnp.zeros((4,) + clip_frames.shape[1:], clip_frames.dtype), clip_frames], axis=0
    )
    bundles = jnp.stack(
        [padded[shift_by : shift_by + frame_count] for shift_by in range(5)], axis=1
    )
    parcels = jnp.einsum(
        "dcf,fkrw->dckrw", outgoing, bundles, preferred_element_type=jnp.float32
    ).astype(jnp.bfloat16)
    arrived = lax.all_to_all(parcels, "span", split_axis=0, concat_axis=0, tiled=True)
    gathered = jnp.einsum(
        "jdc,dckrw->jkrw", incoming, arrived, preferred_element_type=jnp.float32
    ).astype(jnp.bfloat16)
    decoded = residual_block(gathered, gain_one, weight_one, gain_two, weight_two)[:, 0]
    return decoded


def solution(mesh):
    return jax.shard_map(
        local,
        mesh=mesh,
        in_specs=(P("span", None, "tile", None), P(), P(), P(), P(), P(), P()),
        out_specs=P("span", "tile", None),
        check_vma=False,
    )
```

profile of v0, /device:TPU:1, one launch (start us, length us, event | category | flops | bytes accessed | tf_op | source)
XLA Modules:
  0.0 157.0 jit_solution(11481886682850305094)
XLA Ops:
  0.7 0.8 fusion.194
  2.2 1.0 copy.234
  3.6 0.8 convert_bitcast_fusion
  4.4 2.8 %copy.125 = bf16[64,1,5,4,768]{4,3,2,1,0:T(4,128)(2,1)} copy(bf16[64,1,5,4,768]{4,0,3,2,1:T(8,128)(2,1)S(1)} %convert_bitcast_fusion) | data formatting | bytes 3932160 | tf_op jit(solution)/shard_map/convert_element_type | solution.py:104
  7.2 13.6 %all-to-all-start = ((bf16[64,1,5,4,768]{4,3,2,1,0:T(4,128)(2,1)}), bf16[64,1,5,4,768]{4,3,2,1,0:T(4,128)(2,1)S(1)}, u32[]{:S(2)}, u32[]{:S(2)}) async-start(bf16[64,1,5,4,768]{4,3,2,1,0:T(4,128)(2,1)} %copy.125), calls=%async_computation | async-start | bytes 3932160 | tf_op jit(solution)/shard_map/all_to_all | solution.py:105
  21.2 45.2 %all-to-all-done = bf16[64,1,5,4,768]{4,3,2,1,0:T(4,128)(2,1)S(1)} async-done(((bf16[64,1,5,4,768]{4,3,2,1,0:T(4,128)(2,1)}), bf16[64,1,5,4,768]{4,3,2,1,0:T(4,128)(2,1)S(1)}, u32[]{:S(2)}, u32[]{:S(2)}) %all-to-all-start) | async-done | bytes 1966112 | tf_op jit(solution)/shard_map/all_to_all | solution.py:105
  66.4 1.7 %convert_multiply_fusion.1 = (f32[32,5,4,768]{3,0,2,1:T(8,128)}, bf16[32,5,4,768]{3,0,2,1:T(8,128)(2,1)S(1)}) fusion(bf16[64,1,5,4,768]{4,3,2,1,0:T(4,128)(2,1)S(1)} %all-to-all-done, bf16[32,64]{1,0:T(8,128)(2,1)S(1)} %convert_reduce_fusion.1), kind=kOutput, calls=%fused_computation.4 | convolution fusion | flops 64389120 | bytes 4919296 | tf_op jit(solution)/shard_map/jdc,dckrw->jkrw/dot_general | solution.py:106
  68.1 2.3 %mul.63 = f32[32,5,4,2,384]{4,3,0,2,1:T(2,128)S(1)} reshape(f32[32,5,4,768]{3,0,2,1:T(8,128)} %get-tuple-element.16) | data formatting | bytes 3932160 | tf_op jit(solution)/shard_map/mul | solution.py:31
  70.5 0.8 reduce_sum.38
  71.3 0.8 mul.64
  72.2 2.9 %mul.65 = f32[32,5,4,768]{3,0,2,1:T(8,128)} reshape(f32[32,5,4,2,384]{4,3,0,2,1:T(2,128)S(1)} %mul.64) | data formatting | bytes 3932160 | tf_op jit(solution)/shard_map/mul | solution.py:31
  75.0 2.1 %multiply_convert_fusion = bf16[32,5,4,768]{3,0,2,1:T(8,128)(2,1)S(1)} fusion(f32[32,5,4,768]{3,0,2,1:T(8,128)} %mul.65, bf16[32,5,4,768]{3,0,2,1:T(8,128)(2,1)S(1)} %get-tuple-element.17, f32[768]{0:T(1024)S(1)} %mul.68), kind=kLoop, calls=%fused_computation.12 | loop fusion | flops 3932160 | bytes 3935232 | tf_op jit(solution)/shard_map/convert_element_type | solution.py:33
  77.1 0.7 fusion.210
  77.9 2.5 %fusion.46 = f32[32,3,4,2,384]{4,0,3,2,1:T(8,128)} fusion(bf16[5,4,4,2,8,384]{5,4,3,2,1,0:T(8,128)(2,1)S(1)} %bitcast.560, bf16[3,3,3,384,384]{4,3,2,1,0:T(8,128)(2,1)} %param.11), kind=kOutput, calls=%fused_computation.86 | convolution fusion | flops 226492416 | bytes 2457600 | tf_op jit(solution)/shard_map/bfrwc,cd->bfrwd/dot_general | solution.py:54
  80.4 2.5 %fusion.44 = f32[32,3,4,2,384]{4,0,3,2,1:T(8,128)} fusion(bf16[5,4,4,2,8,384]{5,4,3,2,1,0:T(8,128)(2,1)S(1)} %bitcast.561, bf16[3,3,3,384,384]{4,3,2,1,0:T(8,128)(2,1)} %param.11), kind=kOutput, calls=%fused_computation.83 | convolution fusion | flops 226492416 | bytes 2457600 | tf_op jit(solution)/shard_map/bfrwc,cd->bfrwd/dot_general | solution.py:54
  82.9 8.1 %collective-permute-start = (bf16[32,5,1,768]{3,0,2,1:T(8,128)(2,1)S(1)}, bf16[32,5,1,768]{3,0,2,1:T(8,128)(2,1)S(1)}, u32[]{:S(2)}, u32[]{:S(2)}) collective-permute-start(bf16[32,5,1,768]{3,0,2,1:T(8,128)(2,1)S(1)} %get-tuple-element.9), channel_id=1, source_target_pairs={{0,1},{1,2},{2,3},{4,5},{5,6},{6,7},{8,9},{9,10},{10,11},{12,13},{... | collective-permute-start | bytes 737288 | tf_op jit(solution)/shard_map/ppermute | solution.py:17
  91.0 2.1 %collective-permute-start.1 = (bf16[32,5,1,768]{3,0,2,1:T(8,128)(2,1)}, bf16[32,5,1,768]{3,0,2,1:T(8,128)(2,1)}, u32[]{:S(2)}, u32[]{:S(2)}) collective-permute-start(bf16[32,5,1,768]{3,0,2,1:T(8,128)(2,1)} %get-tuple-element.8), channel_id=1, source_target_pairs={{1,0},{2,1},{3,2},{5,4},{6,5},{7,6},{9,8},{10,9},{11,10},{13,12},{... | collective-permute-start | bytes 737288 | tf_op jit(solution)/shard_map/ppermute | solution.py:19
  93.1 2.5 %fusion.42 = f32[32,3,4,2,384]{4,0,3,2,1:T(8,128)} fusion(bf16[5,4,4,2,8,384]{5,4,3,2,1,0:T(8,128)(2,1)S(1)} %bitcast.562, bf16[3,3,3,384,384]{4,3,2,1,0:T(8,128)(2,1)} %param.11), kind=kOutput, calls=%fused_computation.81 | convolution fusion | flops 226492416 | bytes 2457600 | tf_op jit(solution)/shard_map/bfrwc,cd->bfrwd/dot_general | solution.py:54
  95.6 0.8 concatenate.42
  96.3 1.0 copy_dynamic-update-slice_fusion.2
  97.3 1.6 %bitcast_dynamic-update-slice_fusion.1 = (bf16[32,5,5,2,384]{4,0,3,2,1:T(8,128)(2,1)S(1)}, bf16[32,5,5,2,384]{4,0,3,2,1:T(8,128)(2,1)}, bf16[32,5,6,2,384]{4,0,3,2,1:T(8,128)(2,1)S(1)}) fusion(bf16[32,5,5,2,384]{4,0,3,2,1:T(8,128)(2,1)S(1)} %get-tuple-element.12, bf16[5,4,4,2,8,384]{5,4,3,2,1,0:T(8,128)(2,1)S(1)} %bitcast.563, ...), kind=kLoop, calls=%fused_computation.88 | loop fusion | bytes 3932160 | tf_op jit(solution)/shard_map/concatenate | solution.py:15
  98.9 1.0 copy-done.3
  100.3 1.0 concatenate.44
  101.3 0.8 copy_dynamic-update-slice_fusion
  102.1 1.6 %fusion.117 = f32[32,3,4,2,384]{4,0,3,2,1:T(8,128)S(1)} fusion(bf16[32,5,6,2,384]{4,0,3,2,1:T(8,128)(2,1)S(1)} %get-tuple-element.15, bf16[3,3,3,384,384]{4,3,2,1,0:T(8,128)(2,1)} %param.11), kind=kOutput, calls=%fused_computation.162 | convolution fusion | flops 113246208 | bytes 2949120 | tf_op jit(solution)/shard_map/bfrwc,cd->bfrwd/dot_general | solution.py:54
  103.7 1.5 fusion.119
  105.2 1.6 fusion.107
  106.8 1.6 %fusion.109 = f32[32,3,4,2,384]{4,0,3,2,1:T(8,128)S(1)} fusion(bf16[32,5,6,2,384]{4,0,3,2,1:T(8,128)(2,1)S(1)} %get-tuple-element.15, bf16[3,3,3,384,384]{4,3,2,1,0:T(8,128)(2,1)} %param.11), kind=kOutput, calls=%fused_computation.154 | convolution fusion | flops 113246208 | bytes 2949120 | tf_op jit(solution)/shard_map/bfrwc,cd->bfrwd/dot_general | solution.py:54
  108.4 1.5 fusion.113
  109.9 1.5 fusion.121
  111.4 1.5 fusion.105
  114.4 0.8 copy-done
  119.3 0.7 copy-done.5
  120.7 0.7 fusion.29
  124.3 1.0 fusion.34
  125.8 4.8 %collective-permute-start.2 = (bf16[32,3,1,768]{3,0,2,1:T(8,128)(2,1)S(1)}, bf16[32,3,1,768]{3,0,2,1:T(8,128)(2,1)S(1)}, u32[]{:S(2)}, u32[]{:S(2)}) collective-permute-start(bf16[32,3,1,768]{3,0,2,1:T(8,128)(2,1)S(1)} %get-tuple-element.10), channel_id=1, source_target_pairs={{0,1},{1,2},{2,3},{4,5},{5,6},{6,7},{8,9},{9,10},{10,11},{12,13},{... | collective-permute-start | bytes 442376 | tf_op jit(solution)/shard_map/ppermute | solution.py:17
  130.6 1.9 %collective-permute-start.3 = (bf16[32,3,1,768]{3,0,2,1:T(8,128)(2,1)S(1)}, bf16[32,3,1,768]{3,0,2,1:T(8,128)(2,1)S(1)}, u32[]{:S(2)}, u32[]{:S(2)}) collective-permute-start(bf16[32,3,1,768]{3,0,2,1:T(8,128)(2,1)S(1)} %get-tuple-element.11), channel_id=1, source_target_pairs={{1,0},{2,1},{3,2},{5,4},{6,5},{7,6},{9,8},{10,9},{11,10},{13,12},{... | collective-permute-start | bytes 442376 | tf_op jit(solution)/shard_map/ppermute | solution.py:19
  133.1 5.5 %collective-permute-done.3 = bf16[32,3,1,768]{3,0,2,1:T(8,128)(2,1)S(1)} collective-permute-done((bf16[32,3,1,768]{3,0,2,1:T(8,128)(2,1)S(1)}, bf16[32,3,1,768]{3,0,2,1:T(8,128)(2,1)S(1)}, u32[]{:S(2)}, u32[]{:S(2)}) %collective-permute-start.3) | collective-permute-done | bytes 147488 | tf_op jit(solution)/shard_map/ppermute | solution.py:19
  139.0 1.4 fusion.77
  140.3 1.2 convolution_add_fusion.31
  141.6 1.2 convolution_add_fusion.30
  142.8 1.4 convolution_add_fusion.29
  144.2 1.2 convolution_add_fusion.28
  145.5 1.2 convolution_add_fusion.27
  146.7 1.2 convolution_add_fusion.26
  148.0 1.2 convolution_add_fusion.25
  149.2 1.2 convolution_add_fusion.24
  156.1 0.8 copy.145
  (92 shorter events, 18.3 us)
Async XLA Ops:
  2.0 1.5 copy-start.6
  7.2 13.6 %copy-start.9 = (f32[384]{0:T(512)S(1)}, f32[384]{0:T(512)}, u32[]{:S(2)}) copy-start(f32[384]{0:T(512)} %param.10) | copy-start | bytes 4612
  7.2 13.7 %copy-start.7 = (s32[64,41]{0,1:T(8,128)S(1)}, s32[64,41]{0,1:T(8,128)}, u32[]{:S(2)}) copy-start(s32[64,41]{0,1:T(8,128)} %param.9) | copy-start | bytes 31492
  7.2 59.2 %all-to-all-start = ((bf16[64,1,5,4,768]{4,3,2,1,0:T(4,128)(2,1)}), bf16[64,1,5,4,768]{4,3,2,1,0:T(4,128)(2,1)S(1)}, u32[]{:S(2)}, u32[]{:S(2)}) async-start(bf16[64,1,5,4,768]{4,3,2,1,0:T(4,128)(2,1)} %copy.125), calls=%async_computation | async-start | bytes 3932160 | tf_op jit(solution)/shard_map/all_to_all | solution.py:105
  82.9 12.7 %collective-permute-start = (bf16[32,5,1,768]{3,0,2,1:T(8,128)(2,1)S(1)}, bf16[32,5,1,768]{3,0,2,1:T(8,128)(2,1)S(1)}, u32[]{:S(2)}, u32[]{:S(2)}) collective-permute-start(bf16[32,5,1,768]{3,0,2,1:T(8,128)(2,1)S(1)} %get-tuple-element.9), channel_id=1, source_target_pairs={{0,1},{1,2},{2,3},{4,5},{5,6},{6,7},{8,9},{9,10},{10,11},{12,13},{... | collective-permute-start | bytes 737288 | tf_op jit(solution)/shard_map/ppermute | solution.py:17
  91.0 9.3 %collective-permute-start.1 = (bf16[32,5,1,768]{3,0,2,1:T(8,128)(2,1)}, bf16[32,5,1,768]{3,0,2,1:T(8,128)(2,1)}, u32[]{:S(2)}, u32[]{:S(2)}) collective-permute-start(bf16[32,5,1,768]{3,0,2,1:T(8,128)(2,1)} %get-tuple-element.8), channel_id=1, source_target_pairs={{1,0},{2,1},{3,2},{5,4},{6,5},{7,6},{9,8},{10,9},{11,10},{13,12},{... | collective-permute-start | bytes 737288 | tf_op jit(solution)/shard_map/ppermute | solution.py:19
  98.9 1.0 copy-start.3
  102.1 10.8 %slice-start.2 = ((s8[7962624]{0:T(1024)(128)(4,1)}), s8[4194304]{0:T(1024)(128)(4,1)S(1)}, s32[]{:S(2)}) async-start(s8[7962624]{0:T(1024)(128)(4,1)} %bitcast.566), calls=%async_computation.3 | async-start | bytes 8388608
  105.2 4.7 %copy-start.4 = (bf16[32,5,5,2,384]{4,0,3,2,1:T(8,128)(2,1)S(1)}, bf16[32,5,5,2,384]{4,0,3,2,1:T(8,128)(2,1)}, u32[]{:S(2)}) copy-start(bf16[32,5,5,2,384]{4,0,3,2,1:T(8,128)(2,1)} %copy-done.3) | copy-start | bytes 3686404
  106.8 6.1 %slice-start.3 = ((s8[7962624]{0:T(1024)(128)(4,1)}), s8[3768320]{0:T(1024)(128)(4,1)S(1)}, s32[]{:S(2)}) async-start(s8[7962624]{0:T(1024)(128)(4,1)} %bitcast.566), calls=%async_computation.4 | async-start | bytes 7536640
  113.9 1.3 copy-start
  118.8 1.3 copy-start.5
  120.6 1.3 copy-start.2
  122.5 1.3 copy-start.1
  124.3 1.0 copy-start.8
  125.8 7.2 %collective-permute-start.2 = (bf16[32,3,1,768]{3,0,2,1:T(8,128)(2,1)S(1)}, bf16[32,3,1,768]{3,0,2,1:T(8,128)(2,1)S(1)}, u32[]{:S(2)}, u32[]{:S(2)}) collective-permute-start(bf16[32,3,1,768]{3,0,2,1:T(8,128)(2,1)S(1)} %get-tuple-element.10), channel_id=1, source_target_pairs={{0,1},{1,2},{2,3},{4,5},{5,6},{6,7},{8,9},{9,10},{10,11},{12,13},{... | collective-permute-start | bytes 442376 | tf_op jit(solution)/shard_map/ppermute | solution.py:17
  130.6 8.0 %collective-permute-start.3 = (bf16[32,3,1,768]{3,0,2,1:T(8,128)(2,1)S(1)}, bf16[32,3,1,768]{3,0,2,1:T(8,128)(2,1)S(1)}, u32[]{:S(2)}, u32[]{:S(2)}) collective-permute-start(bf16[32,3,1,768]{3,0,2,1:T(8,128)(2,1)S(1)} %get-tuple-element.11), channel_id=1, source_target_pairs={{1,0},{2,1},{3,2},{5,4},{6,5},{7,6},{9,8},{10,9},{11,10},{13,12},{... | collective-permute-start | bytes 442376 | tf_op jit(solution)/shard_map/ppermute | solution.py:19
  138.7 11.8 %slice-start = ((s8[7962624]{0:T(1024)(128)(4,1)}), s8[4194304]{0:T(1024)(128)(4,1)S(1)}, s32[]{:S(2)}) async-start(s8[7962624]{0:T(1024)(128)(4,1)} %bitcast.564), calls=%async_computation.1 | async-start | bytes 8388608
  142.8 7.6 %slice-start.1 = ((s8[7962624]{0:T(1024)(128)(4,1)}), s8[3768320]{0:T(1024)(128)(4,1)S(1)}, s32[]{:S(2)}) async-start(s8[7962624]{0:T(1024)(128)(4,1)} %bitcast.564), calls=%async_computation.2 | async-start | bytes 7536640
where the time goes:
time: 158 us; the launch traced here: 157 us
  waiting for transfers between devices  51.1 us (32%)
  matrix products  46.5 us (29%)
  starting transfers between devices  30.5 us (19%)
  local copies, waits for them, and re-layouts  21.6 us (14%)
  other arithmetic  6.33 us (4%)
    all_to_all x1, waiting for transfers between devices, local(): lax.all_to_all(parcels, 'span', split_axis=0, concat_axis=0, tiled=True)  45.2 us
    dot_general x54, matrix products, causal_conv(): jnp.einsum('bfrwc,cd->bfrwd', window, weight[time_tap, row_tap, column_ta...  44 us
    all_to_all x1, starting transfers between devices, local(): lax.all_to_all(parcels, 'span', split_axis=0, concat_axis=0, tiled=True)  13.6 us
    ppermute x2, starting transfers between devices, with_halo(): lax.ppermute(tail, axis, [(i, (i + 1) % count) for i in range(ends)])  12.9 us
    unnamed x34, local copies, waits for them, and re-layouts  6.02 us
    ppermute x2, waiting for transfers between devices, with_halo(): lax.ppermute(head, axis, [((i + 1) % count, i) for i in range(ends)])  5.89 us
    concatenate x8, local copies, waits for them, and re-layouts, with_halo(): jnp.concatenate([lax.ppermute(tail, axis, [(i, (i + 1) % count) for i in...  4.25 us
    ppermute x2, starting transfers between devices, with_halo(): lax.ppermute(head, axis, [((i + 1) % count, i) for i in range(ends)])  4.02 us
  transfers between devices with their start and end apart: 5, of which 3 were waited for; matrix products, arithmetic and copies ran while one was open for 4% of the time, Pallas kernels for 0%

commit v1 on v0

v1 whole, which is shorter than its diff:
```python
import functools

import jax
import jax.numpy as jnp
from jax import lax
from jax.experimental import pallas as pl
from jax.experimental.pallas import tpu as pltpu
from jax.sharding import PartitionSpec as P

MESH = pl.DeviceIdType.MESH
FRAMES = 41
PAD = 48
ROWS = 4
C = 384
WIDE = 2 * C
WSLOT = 32
SPAN = 64
TILES = 4
TAPS = 9
LANES = 128
GROUPS = WIDE // LANES
F32 = jnp.float32
BF16 = jnp.bfloat16


def activate(values, gain):
    def half(x):
        return jax.nn.silu(x * lax.rsqrt(jnp.mean(x * x, axis=-1, keepdims=True) + 1e-06) * gain)

    return jnp.concatenate([half(values[:, :C]), half(values[:, C:])], axis=1)


def put_shifts(shifted, row, values, own=True):
    frame = lax.broadcasted_iota(jnp.int32, values.shape, 0)
    if own:
        shifted[2, row] = values.astype(BF16)
    shifted[1, row] = jnp.where(frame >= 1, pltpu.roll(values, 1, 0), 0.0).astype(BF16)
    shifted[0, row] = jnp.where(frame >= 2, pltpu.roll(values, 2, 0), 0.0).astype(BF16)


def causal_conv(shifted, weight, total, rows, wait):
    size = rows * PAD
    total[:size] = jnp.zeros((size, WIDE), F32)

    def step(a, carry):
        for b in range(3):
            wait(a * 3 + b)
        lhs = jnp.concatenate([shifted[a, b : b + rows].reshape(size, WIDE) for b in range(3)], axis=1)
        rhs = jnp.concatenate(
            [
                jnp.concatenate([weight[a * 3 + b, C : 3 * C], weight[a * 3 + b, 0 : 2 * C]], axis=1)
                for b in range(3)
            ],
            axis=0,
        )
        total[:size] += jnp.dot(lhs, rhs, preferred_element_type=F32)
        return carry

    lax.fori_loop(0, 3, step, 0)


def kernel(
    feat, slots, gain_one, w_one, gain_two, w_two, out,
    raw, slotv, g1, g2, nat, sh1, sh2, total, v1, v2, send, arrive, pickv, srcv, picks, srcs,
    in_sem, w_sem, smem_sem, halo_send, halo_recv, send_sem, recv_sem,
):
    pos = lax.axis_index("span")
    tile = lax.axis_index("tile")

    inputs = [
        pltpu.make_async_copy(feat, raw, in_sem.at[0]),
        pltpu.make_async_copy(gain_one, g1, in_sem.at[1]),
        pltpu.make_async_copy(slots, slotv, in_sem.at[2]),
        pltpu.make_async_copy(gain_two, g2, in_sem.at[3]),
    ]
    for copy in inputs:
        copy.start()
    for which, (src, dst) in enumerate(((w_one, v1), (w_two, v2))):
        for tap in range(TAPS):
            pltpu.make_async_copy(src.at[tap], dst.at[tap], w_sem.at[which, tap]).start()

    barrier = pltpu.get_barrier_semaphore()

    def greet(k, carry):
        pl.semaphore_signal(
            barrier, inc=1, device_id={"span": lax.rem(pos + k, SPAN), "tile": tile}, device_id_type=MESH
        )
        return carry

    for side in (1, TILES - 1):
        pl.semaphore_signal(
            barrier, inc=1, device_id={"span": pos, "tile": lax.rem(tile + side, TILES)}, device_id_type=MESH
        )
    lax.fori_loop(1, SPAN, greet, 0)

    inputs[0].wait()
    inputs[1].wait()
    for f in range(FRAMES):
        values = raw[f].astype(F32)
        for g in range(GROUPS):
            nat[g, ROWS * f : ROWS * (f + 1), :] = values[:, g * LANES : (g + 1) * LANES]
    nat[:, ROWS * FRAMES :, :] = jnp.zeros((GROUPS, ROWS * (PAD - FRAMES), LANES), F32)
    for r in range(ROWS):
        values = jnp.concatenate([nat[g, pl.ds(r, PAD, stride=ROWS), :] for g in range(GROUPS)], axis=1)
        put_shifts(sh1, 2 + r, activate(values, g1[...].reshape(1, C)))

    pl.semaphore_wait(barrier, SPAN + 1)

    down = pltpu.make_async_remote_copy(
        src_ref=sh1.at[2, pl.ds(4, 2)], dst_ref=sh1.at[2, pl.ds(0, 2)],
        send_sem=halo_send.at[0], recv_sem=halo_recv.at[0],
        device_id={"span": pos, "tile": lax.rem(tile + 1, TILES)}, device_id_type=MESH,
    )
    up = pltpu.make_async_remote_copy(
        src_ref=sh1.at[2, pl.ds(2, 2)], dst_ref=sh1.at[2, pl.ds(6, 2)],
        send_sem=halo_send.at[1], recv_sem=halo_recv.at[1],
        device_id={"span": pos, "tile": lax.rem(tile + TILES - 1, TILES)}, device_id_type=MESH,
    )

    @pl.when(tile < TILES - 1)
    def _():
        down.start()

    @pl.when(tile > 0)
    def _():
        up.start()

    inputs[2].wait()
    inputs[3].wait()
    table = slotv[...]
    lane = lax.broadcasted_iota(jnp.int32, (FRAMES, SPAN), 1)
    column = jnp.sum(jnp.where(lane == pos, table, 0), axis=1, keepdims=True)
    target = jnp.where(column >= 0, column // WSLOT, -1)
    wide_lane = lax.broadcasted_iota(jnp.int32, (FRAMES, 128), 1)
    frame = lax.broadcasted_iota(jnp.int32, (FRAMES, 128), 0)
    pick = jnp.max(jnp.where(target == wide_lane, frame, 0), axis=0, keepdims=True)
    pickv[...] = jnp.broadcast_to(pick, (8, 128))
    wanted = pos * WSLOT + lax.broadcasted_iota(jnp.int32, (WSLOT, SPAN), 0)
    clip = lax.broadcasted_iota(jnp.int32, (WSLOT, SPAN), 1)
    found = jnp.zeros((WSLOT, SPAN), jnp.int32)
    for f in range(FRAMES):
        found = jnp.where(table[f : f + 1, :] == wanted, clip, found)
    srcv[...] = jnp.broadcast_to(jnp.max(found, axis=1, keepdims=True), (WSLOT, 128))
    to_smem = [
        pltpu.make_async_copy(pickv, picks, smem_sem.at[0]),
        pltpu.make_async_copy(srcv, srcs, smem_sem.at[1]),
    ]
    for copy in to_smem:
        copy.start()

    @pl.when(tile > 0)
    def _():
        down.wait_recv()

    @pl.when(tile == 0)
    def _():
        sh1[2, 0:2] = jnp.zeros((2, PAD, WIDE), BF16)

    @pl.when(tile < TILES - 1)
    def _():
        up.wait_recv()

    @pl.when(tile == TILES - 1)
    def _():
        sh1[2, 6:8] = jnp.zeros((2, PAD, WIDE), BF16)

    for row in (0, 1, 6, 7):
        put_shifts(sh1, row, sh1[2, row].astype(F32), own=False)

    def wait_for(which, src, dst):
        def wait(tap):
            pltpu.make_async_copy(src.at[tap], dst.at[tap], w_sem.at[which, tap]).wait()

        return wait

    causal_conv(sh1, v1, total, 6, wait_for(0, w_one, v1))
    for q in range(6):
        values = activate(total[q * PAD : (q + 1) * PAD, :].astype(BF16).astype(F32), g2[...].reshape(1, C))
        if q == 0:
            values = jnp.where(tile == 0, 0.0, values)
        if q == 5:
            values = jnp.where(tile == TILES - 1, 0.0, values)
        put_shifts(sh2, q, values)
    causal_conv(sh2, v2, total, ROWS, wait_for(1, w_two, v2))
    for r in range(ROWS):
        for g in range(GROUPS):
            nat[g, pl.ds(r, PAD, stride=ROWS), :] += total[
                r * PAD : (r + 1) * PAD, g * LANES : (g + 1) * LANES
            ]
    for f in range(FRAMES):
        frame_rows = [nat[g, ROWS * f : ROWS * (f + 1), :] for g in range(GROUPS)]
        raw[f] = jnp.concatenate(frame_rows, axis=1).astype(BF16)

    for copy in to_smem:
        copy.wait()

    def parcel(dest):
        return raw[picks[0, dest]]

    arrive[pos] = parcel(pos)

    def post(k, carry):
        dest = lax.rem(pos + k, SPAN)
        send[dest] = parcel(dest)
        pltpu.make_async_remote_copy(
            src_ref=send.at[dest], dst_ref=arrive.at[pos], send_sem=send_sem, recv_sem=recv_sem,
            device_id={"span": dest, "tile": tile}, device_id_type=MESH,
        ).start()
        return carry

    lax.fori_loop(1, SPAN, post, 0)

    @pl.when(tile < TILES - 1)
    def _():
        down.wait_send()

    @pl.when(tile > 0)
    def _():
        up.wait_send()

    every = pl.ds(0, SPAN - 1)
    pltpu.make_async_copy(send.at[every], send.at[every], send_sem).wait()
    pltpu.make_async_copy(arrive.at[every], arrive.at[every], recv_sem).wait()

    def place(j, carry):
        out[j] = arrive[srcs[j, 0]]
        return carry

    lax.fori_loop(0, WSLOT, place, 0)


def local(features, clip_lengths, slot_table, gain_one, weight_one, gain_two, weight_two):
    del clip_lengths
    hbm = pl.BlockSpec(memory_space=pl.ANY)
    return pl.pallas_call(
        kernel,
        out_shape=jax.ShapeDtypeStruct((WSLOT, ROWS, WIDE), BF16),
        in_specs=[hbm] * 6,
        out_specs=pl.BlockSpec(memory_space=pltpu.VMEM),
        scratch_shapes=[
            pltpu.VMEM((FRAMES, ROWS, WIDE), BF16),
            pltpu.VMEM((FRAMES, SPAN), jnp.int32),
            pltpu.VMEM((C,), F32),
            pltpu.VMEM((C,), F32),
            pltpu.VMEM((GROUPS, ROWS * PAD, LANES), F32),
            pltpu.VMEM((3, 8, PAD, WIDE), BF16),
            pltpu.VMEM((3, 6, PAD, WIDE), BF16),
            pltpu.VMEM((6 * PAD, WIDE), F32),
            pltpu.VMEM((TAPS, 3 * C, C), BF16),
            pltpu.VMEM((TAPS, 3 * C, C), BF16),
            pltpu.VMEM((SPAN, ROWS, WIDE), BF16),
            pltpu.VMEM((SPAN, ROWS, WIDE), BF16),
            pltpu.VMEM((8, 128), jnp.int32),
            pltpu.VMEM((WSLOT, 128), jnp.int32),
            pltpu.SMEM((8, 128), jnp.int32),
            pltpu.SMEM((WSLOT, 128), jnp.int32),
            pltpu.SemaphoreType.DMA((4,)),
            pltpu.SemaphoreType.DMA((2, TAPS)),
            pltpu.SemaphoreType.DMA((2,)),
            pltpu.SemaphoreType.DMA((2,)),
            pltpu.SemaphoreType.DMA((2,)),
            pltpu.SemaphoreType.DMA,
            pltpu.SemaphoreType.DMA,
        ],
        compiler_params=pltpu.CompilerParams(
            collective_id=0, has_side_effects=True, vmem_limit_bytes=60 * 1024 * 1024
        ),
    )(
        features.reshape(FRAMES, ROWS, WIDE),
        slot_table.T,
        gain_one,
        weight_one.reshape(TAPS, 3 * C, C),
        gain_two,
        weight_two.reshape(TAPS, 3 * C, C),
    )


def solution(mesh):
    return jax.shard_map(
        local,
        mesh=mesh,
        in_specs=(P("span", None, "tile", None), P(), P(), P(), P(), P(), P()),
        out_specs=P("span", "tile", None),
        check_vma=False,
    )
```

time: 158 us -> 35.5 us (0.22)
  waiting for transfers between devices: 51.1 us -> 0 us
  matrix products: 46.5 us -> 0 us
  Pallas kernels: 0 us -> 33.7 us
  starting transfers between devices: 30.5 us -> 0 us
  local copies, waits for them, and re-layouts: 21.6 us -> 1.67 us
  other arithmetic: 6.33 us -> 0 us
    dot_general x56 -> x0, matrix products: 46.5 us -> none  [the longest x54 44 us: causal_conv(): jnp.einsum('bfrwc,cd->bfrwd', window, weight[time_tap, row_tap, column_ta...]
    all_to_all x1 -> x0, waiting for transfers between devices: 45.2 us -> none  [local(): lax.all_to_all(parcels, 'span', split_axis=0, concat_axis=0, tiled=True)]
    pallas_call x0 -> x1, Pallas kernels: none -> 33.7 us  [local(): pl.pallas_call(kernel, out_shape=jax.ShapeDtypeStruct((WSLOT, ROWS, WIDE)...]
    ppermute x4 -> x0, starting transfers between devices: 16.9 us -> none  [the longest x2 12.9 us: with_halo(): lax.ppermute(tail, axis, [(i, (i + 1) % count) for i in range(ends)])]
    all_to_all x1 -> x0, starting transfers between devices: 13.6 us -> none  [local(): lax.all_to_all(parcels, 'span', split_axis=0, concat_axis=0, tiled=True)]
    mul x5 -> x0, local copies, waits for them, and re-layouts: 6.06 us -> none  [the longest x4 3.73 us: activate(): shaped * lax.rsqrt(jnp.mean(shaped * shaped, axis=-1, keepdims=True) + 1e...]
    ppermute x4 -> x0, waiting for transfers between devices: 5.89 us -> none  [the longest x2 5.89 us: with_halo(): lax.ppermute(head, axis, [((i + 1) % count, i) for i in range(ends)])]
    unnamed x34 -> x1, local copies, waits for them, and re-layouts: 6.02 us -> 1.67 us
  transfers between devices with their start and end apart: 5 -> 0, of which waited for: 3 -> 0; matrix products, arithmetic and copies ran while one was open for 4% -> 0% of each run, Pallas kernels for 0% -> 0%
where the time goes in v1:
time: 35.5 us; the launch traced here: 35.4 us
  Pallas kernels  33.7 us (95%)
  local copies, waits for them, and re-layouts  1.67 us (5%)
    pallas_call x1, Pallas kernels, local(): pl.pallas_call(kernel, out_shape=jax.ShapeDtypeStruct((WSLOT, ROWS, WIDE)...  33.7 us
    unnamed x1, local copies, waits for them, and re-layouts  1.67 us

profile of v1, /device:TPU:1, one launch (start us, length us, event | category | flops | bytes accessed | tf_op | source)
XLA Modules:
  0.0 35.4 jit_solution(10191768974132835137)
XLA Ops:
  0.0 33.7 %shard_map.64 = bf16[32,4,768]{2,1,0:T(4,128)(2,1)} custom-call(bf16[41,4,768]{2,1,0:T(4,128)(2,1)} %bitcast.6, s32[41,64]{1,0:T(8,128)} %bitcast.7, f32[384]{0:T(512)} %gain_one.1, bf16[9,1152,384]{2,1,0:T(8,128)(2,1)} %bitcast.4, f32[384]{0:T(512)} %gain_two.1, bf16[9,1152,384]{2,1,0:T(8,128)(2,1)} %bitcast.5), custom_call_target="tpu_custom_call" | custom-call | tf_op jit(solution)/shard_map/pallas_call | solution.py:235
  33.8 1.7 %copy.8 = bf16[32,4,768]{2,1,0:T(4,128)(2,1)} copy(bf16[32,4,768]{2,1,0:T(4,128)(2,1)} %shard_map.64) | data formatting | bytes 393216

commit v2 on v1

v2 whole, which is shorter than its diff:
```python
import functools

import jax
import jax.numpy as jnp
from jax import lax
from jax.experimental import pallas as pl
from jax.experimental.pallas import tpu as pltpu
from jax.sharding import PartitionSpec as P

MESH = pl.DeviceIdType.MESH
FRAMES = 41
PAD = 48
ROWS = 4
C = 384
WIDE = 2 * C
WSLOT = 32
SPAN = 64
TILES = 4
TAPS = 9
LANES = 128
GROUPS = WIDE // LANES
F32 = jnp.float32
BF16 = jnp.bfloat16


def activate(values, gain):
    def half(x):
        return jax.nn.silu(x * lax.rsqrt(jnp.mean(x * x, axis=-1, keepdims=True) + 1e-06) * gain)

    return jnp.concatenate([half(values[:, :C]), half(values[:, C:])], axis=1)


def put_shifts(shifted, row, values):
    frame = lax.broadcasted_iota(jnp.int32, values.shape, 0)
    shifted[2, row] = values.astype(BF16)
    shifted[1, row] = jnp.where(frame >= 1, pltpu.roll(values, 1, 0), 0.0).astype(BF16)
    shifted[0, row] = jnp.where(frame >= 2, pltpu.roll(values, 2, 0), 0.0).astype(BF16)


def causal_conv(shifted, first, rows, weight, total):
    size = rows * PAD
    lhs = jnp.concatenate(
        [shifted[a, first + b : first + b + rows].reshape(size, WIDE) for a in range(3) for b in range(3)], axis=1
    )
    for block in range(3):
        rhs = []
        for tap in range(TAPS):
            if block == 0:
                rhs.append(weight[tap, C:, 0:256])
            elif block == 1:
                rhs.append(jnp.concatenate([weight[tap, C:, 256:], weight[tap, : 2 * C, :128]], axis=1))
            else:
                rhs.append(weight[tap, : 2 * C, 128:])
        total[:size, block * 256 : (block + 1) * 256] = jnp.dot(
            lhs, jnp.concatenate(rhs, axis=0), preferred_element_type=F32
        )


def kernel(
    feat, slots, gain_one, w_one, gain_two, w_two, out,
    raw, slotv, g1, g2, nat, mix, sh1, sh2, near, far, total, v1, v2, block, send, arrive, pickv, srcv, picks, srcs,
    in_sem, w_sem, smem_sem, halo_send, halo_recv, send_sem, recv_sem,
):
    pos = lax.axis_index("span")
    tile = lax.axis_index("tile")
    flip = tile // 2
    edge = jnp.where((tile == 0) | (tile == TILES - 1), 1, 0)
    partner = tile + 1 - 2 * lax.rem(tile, 2)
    opposite = TILES - 1 - tile

    def physical(row):
        return row + flip * (ROWS - 1 - 2 * row)

    inputs = [
        pltpu.make_async_copy(feat, raw, in_sem.at[0]),
        pltpu.make_async_copy(gain_one, g1, in_sem.at[1]),
        pltpu.make_async_copy(slots, slotv, in_sem.at[2]),
        pltpu.make_async_copy(gain_two, g2, in_sem.at[3]),
    ]
    for copy in inputs:
        copy.start()
    weights = []
    for which, (src, dst) in enumerate(((w_one, v1), (w_two, v2))):
        for a in range(3):
            for b in range(3):
                tap = a * 3 + b + flip * (2 - 2 * b)
                weights.append(pltpu.make_async_copy(src.at[tap], dst.at[a * 3 + b], w_sem.at[which, a * 3 + b]))
    for copy in weights:
        copy.start()

    barrier = pltpu.get_barrier_semaphore()

    def greet(k, carry):
        pl.semaphore_signal(
            barrier, inc=1, device_id={"span": lax.rem(pos + k, SPAN), "tile": tile}, device_id_type=MESH
        )
        return carry

    for other in (partner, opposite):
        pl.semaphore_signal(barrier, inc=1, device_id={"span": pos, "tile": other}, device_id_type=MESH)
    lax.fori_loop(1, SPAN, greet, 0)

    inputs[0].wait()
    inputs[1].wait()
    for f in range(FRAMES):
        values = raw[f].astype(F32)
        for g in range(GROUPS):
            nat[g, ROWS * f : ROWS * (f + 1), :] = values[:, g * LANES : (g + 1) * LANES]
    nat[:, ROWS * FRAMES :, :] = jnp.zeros((GROUPS, ROWS * (PAD - FRAMES), LANES), F32)

    def own_row(step):
        row = lax.rem(step + 2 * edge, ROWS)
        at = pl.ds(physical(row), PAD, stride=ROWS)
        values = jnp.concatenate([nat[g, at, :] for g in range(GROUPS)], axis=1)
        put_shifts(sh1, 2 + row, activate(values, g1[...].reshape(1, C)))

    own_row(0)
    own_row(1)
    pl.semaphore_wait(barrier, SPAN + 1)
    to_near = pltpu.make_async_remote_copy(
        src_ref=sh1.at[2, pl.ds(2 + 2 * edge, 2)], dst_ref=near, send_sem=halo_send.at[0], recv_sem=halo_recv.at[0],
        device_id={"span": pos, "tile": partner}, device_id_type=MESH,
    )
    to_near.start()
    own_row(2)
    own_row(3)
    to_far = pltpu.make_async_remote_copy(
        src_ref=sh1.at[2, pl.ds(4, 2)], dst_ref=far, send_sem=halo_send.at[1], recv_sem=halo_recv.at[1],
        device_id={"span": pos, "tile": opposite}, device_id_type=MESH,
    )

    @pl.when(edge == 0)
    def _():
        to_far.start()

    inputs[2].wait()
    inputs[3].wait()
    table = slotv[...]
    lane = lax.broadcasted_iota(jnp.int32, (FRAMES, SPAN), 1)
    column = jnp.sum(jnp.where(lane == pos, table, 0), axis=1, keepdims=True)
    target = jnp.where(column >= 0, column // WSLOT, -1)
    wide_lane = lax.broadcasted_iota(jnp.int32, (FRAMES, 128), 1)
    frame = lax.broadcasted_iota(jnp.int32, (FRAMES, 128), 0)
    pick = jnp.max(jnp.where(target == wide_lane, frame, 0), axis=0, keepdims=True)
    pickv[...] = jnp.broadcast_to(pick, (8, 128))
    wanted = pos * WSLOT + lax.broadcasted_iota(jnp.int32, (WSLOT, SPAN), 0)
    clip = lax.broadcasted_iota(jnp.int32, (WSLOT, SPAN), 1)
    found = jnp.zeros((WSLOT, SPAN), jnp.int32)
    for f in range(FRAMES):
        found = jnp.where(table[f : f + 1, :] == wanted, clip, found)
    srcv[...] = jnp.broadcast_to(jnp.max(found, axis=1, keepdims=True), (WSLOT, 128))
    to_smem = [
        pltpu.make_async_copy(pickv, picks, smem_sem.at[0]),
        pltpu.make_async_copy(srcv, srcs, smem_sem.at[1]),
    ]
    for copy in to_smem:
        copy.start()

    @pl.when(edge == 1)
    def _():
        sh1[:, 0:2] = jnp.zeros((3, 2, PAD, WIDE), BF16)

    @pl.when(edge == 0)
    def _():
        to_near.wait_recv()
        for row in range(2):
            put_shifts(sh1, row, near[row].astype(F32))

    def hidden_rows(first, rows):
        for i in range(rows):
            values = activate(total[i * PAD : (i + 1) * PAD, :].astype(BF16).astype(F32), g2[...].reshape(1, C))
            if first + i == 0:
                values = jnp.where(edge == 1, 0.0, values)
            put_shifts(sh2, first + i, values)

    def emit(half):
        part = half + flip * (1 - 2 * half)
        for i in range(2):
            row = physical(2 * half + i)
            for g in range(GROUPS):
                mix[g, pl.ds(lax.rem(row, 2), PAD, stride=2), :] = (
                    nat[g, pl.ds(row, PAD, stride=ROWS), :]
                    + total[i * PAD : (i + 1) * PAD, g * LANES : (g + 1) * LANES]
                )
        for f in range(FRAMES):
            block[f] = jnp.concatenate([mix[g, 2 * f : 2 * f + 2, :] for g in range(GROUPS)], axis=1).astype(BF16)
        arrive[part, pos] = block[picks[0, pos]]

        def post(k, carry):
            dest = lax.rem(pos + k, SPAN)
            send[part, dest] = block[picks[0, dest]]
            pltpu.make_async_remote_copy(
                src_ref=send.at[part, dest], dst_ref=arrive.at[part, pos],
                send_sem=send_sem.at[half], recv_sem=recv_sem.at[half],
                device_id={"span": dest, "tile": tile}, device_id_type=MESH,
            ).start()
            return carry

        lax.fori_loop(1, SPAN, post, 0)

    for copy in weights[:TAPS]:
        copy.wait()
    causal_conv(sh1, 0, 4, v1, total)
    hidden_rows(0, 4)
    for copy in weights[TAPS:]:
        copy.wait()
    causal_conv(sh2, 0, 2, v2, total)
    for copy in to_smem:
        copy.wait()
    emit(0)

    @pl.when(edge == 1)
    def _():
        to_near.wait_recv()
        for row in range(2):
            put_shifts(sh1, 6 + row, near[row].astype(F32))

    @pl.when(edge == 0)
    def _():
        to_far.wait_recv()
        for row in range(2):
            put_shifts(sh1, 7 - row, far[row].astype(F32))

    causal_conv(sh1, 4, 2, v1, total)
    hidden_rows(4, 2)
    causal_conv(sh2, 2, 2, v2, total)
    emit(1)

    to_near.wait_send()

    @pl.when(edge == 0)
    def _():
        to_far.wait_send()

    every = pl.ds(0, SPAN - 1)
    for half in range(2):
        pltpu.make_async_copy(send.at[half, every], send.at[half, every], send_sem.at[half]).wait()
        pltpu.make_async_copy(arrive.at[half, every], arrive.at[half, every], recv_sem.at[half]).wait()

    def place(j, carry):
        clip = srcs[j, 0]
        out[j] = jnp.concatenate([arrive[0, clip], arrive[1, clip]], axis=0)
        return carry

    lax.fori_loop(0, WSLOT, place, 0)


def local(features, clip_lengths, slot_table, gain_one, weight_one, gain_two, weight_two):
    del clip_lengths
    hbm = pl.BlockSpec(memory_space=pl.ANY)
    return pl.pallas_call(
        kernel,
        out_shape=jax.ShapeDtypeStruct((WSLOT, ROWS, WIDE), BF16),
        in_specs=[hbm] * 6,
        out_specs=pl.BlockSpec(memory_space=pltpu.VMEM),
        scratch_shapes=[
            pltpu.VMEM((FRAMES, ROWS, WIDE), BF16),
            pltpu.VMEM((FRAMES, SPAN), jnp.int32),
            pltpu.VMEM((C,), F32),
            pltpu.VMEM((C,), F32),
            pltpu.VMEM((GROUPS, ROWS * PAD, LANES), F32),
            pltpu.VMEM((GROUPS, 2 * PAD, LANES), F32),
            pltpu.VMEM((3, 8, PAD, WIDE), BF16),
            pltpu.VMEM((3, 6, PAD, WIDE), BF16),
            pltpu.VMEM((2, PAD, WIDE), BF16),
            pltpu.VMEM((2, PAD, WIDE), BF16),
            pltpu.VMEM((4 * PAD, WIDE), F32),
            pltpu.VMEM((TAPS, 3 * C, C), BF16),
            pltpu.VMEM((TAPS, 3 * C, C), BF16),
            pltpu.VMEM((FRAMES, 2, WIDE), BF16),
            pltpu.VMEM((2, SPAN, 2, WIDE), BF16),
            pltpu.VMEM((2, SPAN, 2, WIDE), BF16),
            pltpu.VMEM((8, 128), jnp.int32),
            pltpu.VMEM((WSLOT, 128), jnp.int32),
            pltpu.SMEM((8, 128), jnp.int32),
            pltpu.SMEM((WSLOT, 128), jnp.int32),
            pltpu.SemaphoreType.DMA((4,)),
            pltpu.SemaphoreType.DMA((2, TAPS)),
            pltpu.SemaphoreType.DMA((2,)),
            pltpu.SemaphoreType.DMA((2,)),
            pltpu.SemaphoreType.DMA((2,)),
            pltpu.SemaphoreType.DMA((2,)),
            pltpu.SemaphoreType.DMA((2,)),
        ],
        compiler_params=pltpu.CompilerParams(
            collective_id=0, has_side_effects=True, vmem_limit_bytes=60 * 1024 * 1024
        ),
    )(
        features.reshape(FRAMES, ROWS, WIDE),
        slot_table.T,
        gain_one,
        weight_one.reshape(TAPS, 3 * C, C),
        gain_two,
        weight_two.reshape(TAPS, 3 * C, C),
    )


def solution(mesh):
    return jax.shard_map(
        local,
        mesh=mesh,
        in_specs=(P("span", None, "tile", None), P(), P(), P(), P(), P(), P()),
        out_specs=P("span", "tile", None),
        check_vma=False,
    )
```

time: 35.5 us -> 34.1 us (0.961)
  Pallas kernels: 33.7 us -> 32.3 us
    pallas_call x1, Pallas kernels: 33.7 us -> 32.3 us  [local(): pl.pallas_call(kernel, out_shape=jax.ShapeDtypeStruct((WSLOT, ROWS, WIDE)...]
where the time goes in v2:
time: 34.1 us; the launch traced here: 34 us
  Pallas kernels  32.3 us (95%)
  local copies, waits for them, and re-layouts  1.67 us (5%)
    pallas_call x1, Pallas kernels, local(): pl.pallas_call(kernel, out_shape=jax.ShapeDtypeStruct((WSLOT, ROWS, WIDE)...  32.3 us
    unnamed x1, local copies, waits for them, and re-layouts  1.67 us

profile of v2, /device:TPU:1, one launch (start us, length us, event | category | flops | bytes accessed | tf_op | source)
XLA Modules:
  0.0 34.0 jit_solution(2609471957769487439)
XLA Ops:
  0.0 32.3 %shard_map.64 = bf16[32,4,768]{2,1,0:T(4,128)(2,1)} custom-call(bf16[41,4,768]{2,1,0:T(4,128)(2,1)} %bitcast.6, s32[41,64]{1,0:T(8,128)} %bitcast.7, f32[384]{0:T(512)} %gain_one.1, bf16[9,1152,384]{2,1,0:T(8,128)(2,1)} %bitcast.4, f32[384]{0:T(512)} %gain_two.1, bf16[9,1152,384]{2,1,0:T(8,128)(2,1)} %bitcast.5), custom_call_target="tpu_custom_call" | custom-call | tf_op jit(solution)/shard_map/pallas_call | solution.py:251
  32.3 1.7 %copy.8 = bf16[32,4,768]{2,1,0:T(4,128)(2,1)} copy(bf16[32,4,768]{2,1,0:T(4,128)(2,1)} %shard_map.64) | data formatting | bytes 393216

commit v3 on v2

--- a/solution.py
+++ b/solution.py
@@ -17,6 +17,14 @@
 SPAN = 64
 TILES = 4
 TAPS = 9
+ACROSS = 4
+DEPTH = 8
+ORDER = [
+    (dy, dx, dz)
+    for dy, dx in ((1, 2), (0, 2), (1, 1), (1, 3), (0, 1), (0, 3), (1, 0), (0, 0))
+    for dz in (4, 3, 5, 2, 6, 1, 7, 0)
+][: SPAN - 1]
+EACH = 8
 LANES = 128
 GROUPS = WIDE // LANES
 F32 = jnp.float32
@@ -37,23 +45,30 @@
     shifted[0, row] = jnp.where(frame >= 2, pltpu.roll(values, 2, 0), 0.0).astype(BF16)
 
 
-def causal_conv(shifted, first, rows, weight, total):
+def product(shifted, pieces, rows, weight, total, start, add=False, between=None):
     size = rows * PAD
     lhs = jnp.concatenate(
-        [shifted[a, first + b : first + b + rows].reshape(size, WIDE) for a in range(3) for b in range(3)], axis=1
+        [shifted[a, first : first + rows].reshape(size, WIDE) for a, b, first in pieces], axis=1
     )
     for block in range(3):
         rhs = []
-        for tap in range(TAPS):
+        for a, b, _ in pieces:
+            tap = a * 3 + b
             if block == 0:
                 rhs.append(weight[tap, C:, 0:256])
             elif block == 1:
                 rhs.append(jnp.concatenate([weight[tap, C:, 256:], weight[tap, : 2 * C, :128]], axis=1))
             else:
                 rhs.append(weight[tap, : 2 * C, 128:])
-        total[:size, block * 256 : (block + 1) * 256] = jnp.dot(
-            lhs, jnp.concatenate(rhs, axis=0), preferred_element_type=F32
-        )
+        result = jnp.dot(lhs, jnp.concatenate(rhs, axis=0), preferred_element_type=F32)
+        at = (slice(start * PAD, start * PAD + size), slice(block * 256, (block + 1) * 256))
+        total[at] = total[at] + result if add else result
+        if between is not None:
+            between()
+
+
+def taps(row_taps, first):
+    return [(a, b, first + b) for a in range(3) for b in row_taps]
 
 
 def kernel(
@@ -156,25 +171,13 @@
     for copy in to_smem:
         copy.start()
 
-    @pl.when(edge == 1)
-    def _():
-        sh1[:, 0:2] = jnp.zeros((3, 2, PAD, WIDE), BF16)
-
-    @pl.when(edge == 0)
-    def _():
-        to_near.wait_recv()
-        for row in range(2):
-            put_shifts(sh1, row, near[row].astype(F32))
-
-    def hidden_rows(first, rows):
-        for i in range(rows):
-            values = activate(total[i * PAD : (i + 1) * PAD, :].astype(BF16).astype(F32), g2[...].reshape(1, C))
-            if first + i == 0:
-                values = jnp.where(edge == 1, 0.0, values)
-            put_shifts(sh2, first + i, values)
-
-    def emit(half):
-        part = half + flip * (1 - 2 * half)
+    def hidden_row(row, start):
+        values = activate(total[start * PAD : (start + 1) * PAD, :].astype(BF16).astype(F32), g2[...].reshape(1, C))
+        if row == 0:
+            values = jnp.where(edge == 1, 0.0, values)
+        put_shifts(sh2, row, values)
+
+    def prepare(half):
         for i in range(2):
             row = physical(2 * half + i)
             for g in range(GROUPS):
@@ -183,31 +186,54 @@
                     + total[i * PAD : (i + 1) * PAD, g * LANES : (g + 1) * LANES]
                 )
         for f in range(FRAMES):
-            block[f] = jnp.concatenate([mix[g, 2 * f : 2 * f + 2, :] for g in range(GROUPS)], axis=1).astype(BF16)
-        arrive[part, pos] = block[picks[0, pos]]
-
-        def post(k, carry):
-            dest = lax.rem(pos + k, SPAN)
-            send[part, dest] = block[picks[0, dest]]
+            block[half, f] = jnp.concatenate([mix[g, 2 * f : 2 * f + 2, :] for g in range(GROUPS)], axis=1).astype(BF16)
+        arrive[half + flip * (1 - 2 * half), pos] = block[half, picks[0, pos]]
+
+    z, x, y = lax.rem(pos, DEPTH), lax.rem(pos // DEPTH, ACROSS), pos // (DEPTH * ACROSS)
+
+    def posts(half, count):
+        part = half + flip * (1 - 2 * half)
+        done = 0
+        for dy, dx, dz in ORDER:
+            dest = (lax.rem(y + dy, 2) * ACROSS + lax.rem(x + dx, ACROSS)) * DEPTH + lax.rem(z + dz, DEPTH)
+            send[part, dest] = block[half, picks[0, dest]]
             pltpu.make_async_remote_copy(
                 src_ref=send.at[part, dest], dst_ref=arrive.at[part, pos],
                 send_sem=send_sem.at[half], recv_sem=recv_sem.at[half],
                 device_id={"span": dest, "tile": tile}, device_id_type=MESH,
             ).start()
-            return carry
-
-        lax.fori_loop(1, SPAN, post, 0)
+            done += 1
+            if done % count == 0:
+                yield
+        while True:
+            yield
 
     for copy in weights[:TAPS]:
         copy.wait()
-    causal_conv(sh1, 0, 4, v1, total)
-    hidden_rows(0, 4)
+    product(sh1, taps((2,), 0), 4, v1, total, 0)
+    product(sh1, taps((0, 1), 2), 2, v1, total, 2, add=True)
+    hidden_row(2, 2)
+    hidden_row(3, 3)
+
+    @pl.when(edge == 1)
+    def _():
+        sh1[:, 0:2] = jnp.zeros((3, 2, PAD, WIDE), BF16)
+
+    @pl.when(edge == 0)
+    def _():
+        to_near.wait_recv()
+        for row in range(2):
+            put_shifts(sh1, row, near[row].astype(F32))
+
+    product(sh1, taps((0, 1), 0), 2, v1, total, 0, add=True)
+    hidden_row(0, 0)
+    hidden_row(1, 1)
     for copy in weights[TAPS:]:
         copy.wait()
-    causal_conv(sh2, 0, 2, v2, total)
+    product(sh2, taps((0, 1, 2), 0), 2, v2, total, 0)
     for copy in to_smem:
         copy.wait()
-    emit(0)
+    prepare(0)
 
     @pl.when(edge == 1)
     def _():
@@ -221,10 +247,19 @@
         for row in range(2):
             put_shifts(sh1, 7 - row, far[row].astype(F32))
 
-    causal_conv(sh1, 4, 2, v1, total)
-    hidden_rows(4, 2)
-    causal_conv(sh2, 2, 2, v2, total)
-    emit(1)
+    first_half = posts(0, EACH)
+
+    def some():
+        next(first_half)
+
+    some()
+    product(sh1, taps((0, 1, 2), 4), 2, v1, total, 0, between=some)
+    hidden_row(4, 0)
+    some()
+    hidden_row(5, 1)
+    product(sh2, taps((0, 1, 2), 2), 2, v2, total, 0, between=some)
+    prepare(1)
+    next(posts(1, SPAN))
 
     to_near.wait_send()
 
@@ -247,10 +282,19 @@
 
 def local(features, clip_lengths, slot_table, gain_one, weight_one, gain_two, weight_two):
     del clip_lengths
-    hbm = pl.BlockSpec(memory_space=pl.ANY)
+    hbm = pl.BlockSpec(memory_space=pltpu.HBM)
+    operands = [
+        features.reshape(FRAMES, ROWS, WIDE),
+        slot_table.T,
+        gain_one,
+        weight_one.reshape(TAPS, 3 * C, C),
+        gain_two,
+        weight_two.reshape(TAPS, 3 * C, C),
+    ]
+    operands = [pltpu.with_memory_space_constraint(x, pltpu.HBM) for x in operands]
     return pl.pallas_call(
         kernel,
-        out_shape=jax.ShapeDtypeStruct((WSLOT, ROWS, WIDE), BF16),
+        out_shape=pltpu.VMEM((WSLOT, ROWS, WIDE), BF16),
         in_specs=[hbm] * 6,
         out_specs=pl.BlockSpec(memory_space=pltpu.VMEM),
         scratch_shapes=[
@@ -267,7 +311,7 @@
             pltpu.VMEM((4 * PAD, WIDE), F32),
             pltpu.VMEM((TAPS, 3 * C, C), BF16),
             pltpu.VMEM((TAPS, 3 * C, C), BF16),
-            pltpu.VMEM((FRAMES, 2, WIDE), BF16),
+            pltpu.VMEM((2, FRAMES, 2, WIDE), BF16),
             pltpu.VMEM((2, SPAN, 2, WIDE), BF16),
             pltpu.VMEM((2, SPAN, 2, WIDE), BF16),
             pltpu.VMEM((8, 128), jnp.int32),
@@ -283,16 +327,9 @@
             pltpu.SemaphoreType.DMA((2,)),
         ],
         compiler_params=pltpu.CompilerParams(
-            collective_id=0, has_side_effects=True, vmem_limit_bytes=60 * 1024 * 1024
+            collective_id=0, has_side_effects=True, vmem_limit_bytes=48 * 1024 * 1024
         ),
-    )(
-        features.reshape(FRAMES, ROWS, WIDE),
-        slot_table.T,
-        gain_one,
-        weight_one.reshape(TAPS, 3 * C, C),
-        gain_two,
-        weight_two.reshape(TAPS, 3 * C, C),
-    )
+    )(*operands)
 
 
 def solution(mesh):

time: 34.1 us -> 33.5 us (0.982)
  local copies, waits for them, and re-layouts: 1.67 us -> 0.68 us
    unnamed x1, local copies, waits for them, and re-layouts: 1.67 us -> 0.68 us
where the time goes in v3:
time: 33.5 us; the launch traced here: 33.3 us
  Pallas kernels  32.6 us (97%)
  local copies, waits for them, and re-layouts  0.68 us (2%)
    pallas_call x1, Pallas kernels, local(): pl.pallas_call(kernel, out_shape=pltpu.VMEM((WSLOT, ROWS, WIDE), BF16), i...  32.6 us
    unnamed x1, local copies, waits for them, and re-layouts  0.68 us

profile of v3, /device:TPU:1, one launch (start us, length us, event | category | flops | bytes accessed | tf_op | source)
XLA Modules:
  0.0 33.3 jit_solution(6083254578606010431)
XLA Ops:
  0.0 32.6 %shard_map.64 = bf16[32,4,768]{2,1,0:T(4,128)(2,1)S(1)} custom-call(bf16[41,4,768]{2,1,0:T(4,128)(2,1)} %bitcast.6, s32[41,64]{1,0:T(8,128)} %bitcast.7, f32[384]{0:T(512)} %gain_one.1, bf16[9,1152,384]{2,1,0:T(8,128)(2,1)} %bitcast.4, f32[384]{0:T(512)} %gain_two.1, bf16[9,1152,384]{2,1,0:T(8,128)(2,1)} %bitcast.5), custom_call_target="tpu_custom_call" | custom-call | tf_op jit(solution)/shard_map/pallas_call | solution.py:295
  32.6 0.7 %copy.8 = bf16[32,4,768]{2,1,0:T(4,128)(2,1)} copy(bf16[32,4,768]{2,1,0:T(4,128)(2,1)S(1)} %shard_map.64) | data formatting | bytes 393216

commit v4 on v3

--- a/solution.py
+++ b/solution.py
@@ -24,7 +24,6 @@
     for dy, dx in ((1, 2), (0, 2), (1, 1), (1, 3), (0, 1), (0, 3), (1, 0), (0, 0))
     for dz in (4, 3, 5, 2, 6, 1, 7, 0)
 ][: SPAN - 1]
-EACH = 8
 LANES = 128
 GROUPS = WIDE // LANES
 F32 = jnp.float32
@@ -45,7 +44,7 @@
     shifted[0, row] = jnp.where(frame >= 2, pltpu.roll(values, 2, 0), 0.0).astype(BF16)
 
 
-def product(shifted, pieces, rows, weight, total, start, add=False, between=None):
+def product(shifted, pieces, rows, weight, total, start, add=False):
     size = rows * PAD
     lhs = jnp.concatenate(
         [shifted[a, first : first + rows].reshape(size, WIDE) for a, b, first in pieces], axis=1
@@ -63,8 +62,6 @@
         result = jnp.dot(lhs, jnp.concatenate(rhs, axis=0), preferred_element_type=F32)
         at = (slice(start * PAD, start * PAD + size), slice(block * 256, (block + 1) * 256))
         total[at] = total[at] + result if add else result
-        if between is not None:
-            between()
 
 
 def taps(row_taps, first):
@@ -191,9 +188,8 @@
 
     z, x, y = lax.rem(pos, DEPTH), lax.rem(pos // DEPTH, ACROSS), pos // (DEPTH * ACROSS)
 
-    def posts(half, count):
+    def post(half):
         part = half + flip * (1 - 2 * half)
-        done = 0
         for dy, dx, dz in ORDER:
             dest = (lax.rem(y + dy, 2) * ACROSS + lax.rem(x + dx, ACROSS)) * DEPTH + lax.rem(z + dz, DEPTH)
             send[part, dest] = block[half, picks[0, dest]]
@@ -202,11 +198,6 @@
                 send_sem=send_sem.at[half], recv_sem=recv_sem.at[half],
                 device_id={"span": dest, "tile": tile}, device_id_type=MESH,
             ).start()
-            done += 1
-            if done % count == 0:
-                yield
-        while True:
-            yield
 
     for copy in weights[:TAPS]:
         copy.wait()
@@ -234,6 +225,7 @@
     for copy in to_smem:
         copy.wait()
     prepare(0)
+    post(0)
 
     @pl.when(edge == 1)
     def _():
@@ -247,19 +239,12 @@
         for row in range(2):
             put_shifts(sh1, 7 - row, far[row].astype(F32))
 
-    first_half = posts(0, EACH)
-
-    def some():
-        next(first_half)
-
-    some()
-    product(sh1, taps((0, 1, 2), 4), 2, v1, total, 0, between=some)
+    product(sh1, taps((0, 1, 2), 4), 2, v1, total, 0)
     hidden_row(4, 0)
-    some()
     hidden_row(5, 1)
-    product(sh2, taps((0, 1, 2), 2), 2, v2, total, 0, between=some)
+    product(sh2, taps((0, 1, 2), 2), 2, v2, total, 0)
     prepare(1)
-    next(posts(1, SPAN))
+    post(1)
 
     to_near.wait_send()
 

time: 33.5 us -> 31 us (0.925)
  Pallas kernels: 32.6 us -> 29.8 us
    pallas_call x1, Pallas kernels: 32.6 us -> 29.8 us  [local(): pl.pallas_call(kernel, out_shape=pltpu.VMEM((WSLOT, ROWS, WIDE), BF16), i...]
where the time goes in v4:
time: 31 us; the launch traced here: 30.5 us
  Pallas kernels  29.8 us (96%)
  local copies, waits for them, and re-layouts  0.68 us (2%)
    pallas_call x1, Pallas kernels, local(): pl.pallas_call(kernel, out_shape=pltpu.VMEM((WSLOT, ROWS, WIDE), BF16), i...  29.8 us
    unnamed x1, local copies, waits for them, and re-layouts  0.68 us

profile of v4, /device:TPU:1, one launch (start us, length us, event | category | flops | bytes accessed | tf_op | source)
XLA Modules:
  0.0 30.5 jit_solution(3606550857460541153)
XLA Ops:
  0.0 29.8 %shard_map.64 = bf16[32,4,768]{2,1,0:T(4,128)(2,1)S(1)} custom-call(bf16[41,4,768]{2,1,0:T(4,128)(2,1)} %bitcast.6, s32[41,64]{1,0:T(8,128)} %bitcast.7, f32[384]{0:T(512)} %gain_one.1, bf16[9,1152,384]{2,1,0:T(8,128)(2,1)} %bitcast.4, f32[384]{0:T(512)} %gain_two.1, bf16[9,1152,384]{2,1,0:T(8,128)(2,1)} %bitcast.5), custom_call_target="tpu_custom_call" | custom-call | tf_op jit(solution)/shard_map/pallas_call | solution.py:280
  29.8 0.7 %copy.8 = bf16[32,4,768]{2,1,0:T(4,128)(2,1)} copy(bf16[32,4,768]{2,1,0:T(4,128)(2,1)S(1)} %shard_map.64) | data formatting | bytes 393216

commit v5 on v4

--- a/solution.py
+++ b/solution.py
@@ -32,7 +32,9 @@
 
 def activate(values, gain):
     def half(x):
-        return jax.nn.silu(x * lax.rsqrt(jnp.mean(x * x, axis=-1, keepdims=True) + 1e-06) * gain)
+        u = x * lax.rsqrt(jnp.mean(x * x, axis=-1, keepdims=True) + 1e-06) * gain
+        half_u = 0.5 * u
+        return half_u + half_u * jnp.tanh(half_u)
 
     return jnp.concatenate([half(values[:, :C]), half(values[:, C:])], axis=1)
 
@@ -70,12 +72,13 @@
 
 def kernel(
     feat, slots, gain_one, w_one, gain_two, w_two, out,
-    raw, slotv, g1, g2, nat, mix, sh1, sh2, near, far, total, v1, v2, block, send, arrive, pickv, srcv, picks, srcs,
-    in_sem, w_sem, smem_sem, halo_send, halo_recv, send_sem, recv_sem,
+    raw, slotv, g1, g2, nat, mix, sh1, sh2, near, far, total, v1, v2, block, send, arrive_one, arrive_two, pickv, srcv, picks, srcs,
+    in_sem, w_sem, smem_sem, halo_send, halo_recv, send_sem, recv_sem, lines_sem, planes_sem,
 ):
     pos = lax.axis_index("span")
     tile = lax.axis_index("tile")
     flip = tile // 2
+    arrive = (arrive_one, arrive_two)
     edge = jnp.where((tile == 0) | (tile == TILES - 1), 1, 0)
     partner = tile + 1 - 2 * lax.rem(tile, 2)
     opposite = TILES - 1 - tile
@@ -89,28 +92,30 @@
         pltpu.make_async_copy(slots, slotv, in_sem.at[2]),
         pltpu.make_async_copy(gain_two, g2, in_sem.at[3]),
     ]
-    for copy in inputs:
-        copy.start()
     weights = []
     for which, (src, dst) in enumerate(((w_one, v1), (w_two, v2))):
         for a in range(3):
             for b in range(3):
                 tap = a * 3 + b + flip * (2 - 2 * b)
                 weights.append(pltpu.make_async_copy(src.at[tap], dst.at[a * 3 + b], w_sem.at[which, a * 3 + b]))
-    for copy in weights:
+    for copy in inputs[:2]:
         copy.start()
 
+    z, x, y = lax.rem(pos, DEPTH), lax.rem(pos // DEPTH, ACROSS), pos // (DEPTH * ACROSS)
+
+    def shifted_by(dy, dx, dz):
+        return (lax.rem(y + dy, 2) * ACROSS + lax.rem(x + dx, ACROSS)) * DEPTH + lax.rem(z + dz, DEPTH)
+
     barrier = pltpu.get_barrier_semaphore()
-
-    def greet(k, carry):
-        pl.semaphore_signal(
-            barrier, inc=1, device_id={"span": lax.rem(pos + k, SPAN), "tile": tile}, device_id_type=MESH
-        )
-        return carry
-
+    along_z = [shifted_by(0, 0, k) for k in range(1, DEPTH)]
+    along_x = [shifted_by(0, k, 0) for k in range(1, ACROSS)]
+    along_y = [shifted_by(1, 0, 0)]
     for other in (partner, opposite):
         pl.semaphore_signal(barrier, inc=1, device_id={"span": pos, "tile": other}, device_id_type=MESH)
-    lax.fori_loop(1, SPAN, greet, 0)
+    for other in along_z + along_x + along_y:
+        pl.semaphore_signal(barrier, inc=1, device_id={"span": other, "tile": tile}, device_id_type=MESH)
+    for copy in weights[:TAPS] + inputs[2:] + weights[TAPS:]:
+        copy.start()
 
     inputs[0].wait()
     inputs[1].wait()
@@ -128,12 +133,14 @@
 
     own_row(0)
     own_row(1)
-    pl.semaphore_wait(barrier, SPAN + 1)
+    pl.semaphore_wait(barrier, 2 + len(along_z) + len(along_x) + len(along_y))
     to_near = pltpu.make_async_remote_copy(
         src_ref=sh1.at[2, pl.ds(2 + 2 * edge, 2)], dst_ref=near, send_sem=halo_send.at[0], recv_sem=halo_recv.at[0],
         device_id={"span": pos, "tile": partner}, device_id_type=MESH,
     )
     to_near.start()
+    for other in along_x:
+        pl.semaphore_signal(lines_sem, inc=1, device_id={"span": other, "tile": tile}, device_id_type=MESH)
     own_row(2)
     own_row(3)
     to_far = pltpu.make_async_remote_copy(
@@ -184,17 +191,14 @@
                 )
         for f in range(FRAMES):
             block[half, f] = jnp.concatenate([mix[g, 2 * f : 2 * f + 2, :] for g in range(GROUPS)], axis=1).astype(BF16)
-        arrive[half + flip * (1 - 2 * half), pos] = block[half, picks[0, pos]]
-
-    z, x, y = lax.rem(pos, DEPTH), lax.rem(pos // DEPTH, ACROSS), pos // (DEPTH * ACROSS)
+        arrive[half][pos] = block[half, picks[0, pos]]
 
     def post(half):
-        part = half + flip * (1 - 2 * half)
         for dy, dx, dz in ORDER:
-            dest = (lax.rem(y + dy, 2) * ACROSS + lax.rem(x + dx, ACROSS)) * DEPTH + lax.rem(z + dz, DEPTH)
-            send[part, dest] = block[half, picks[0, dest]]
+            dest = shifted_by(dy, dx, dz)
+            send[half, dest] = block[half, picks[0, dest]]
             pltpu.make_async_remote_copy(
-                src_ref=send.at[part, dest], dst_ref=arrive.at[part, pos],
+                src_ref=send.at[half, dest], dst_ref=arrive[half].at[pos],
                 send_sem=send_sem.at[half], recv_sem=recv_sem.at[half],
                 device_id={"span": dest, "tile": tile}, device_id_type=MESH,
             ).start()
@@ -202,9 +206,9 @@
     for copy in weights[:TAPS]:
         copy.wait()
     product(sh1, taps((2,), 0), 4, v1, total, 0)
-    product(sh1, taps((0, 1), 2), 2, v1, total, 2, add=True)
-    hidden_row(2, 2)
-    hidden_row(3, 3)
+    pl.semaphore_wait(lines_sem, len(along_x))
+    for other in along_y:
+        pl.semaphore_signal(planes_sem, inc=1, device_id={"span": other, "tile": tile}, device_id_type=MESH)
 
     @pl.when(edge == 1)
     def _():
@@ -216,15 +220,16 @@
         for row in range(2):
             put_shifts(sh1, row, near[row].astype(F32))
 
-    product(sh1, taps((0, 1), 0), 2, v1, total, 0, add=True)
-    hidden_row(0, 0)
-    hidden_row(1, 1)
+    product(sh1, taps((0, 1), 0), 4, v1, total, 0, add=True)
+    for row in range(4):
+        hidden_row(row, row)
     for copy in weights[TAPS:]:
         copy.wait()
     product(sh2, taps((0, 1, 2), 0), 2, v2, total, 0)
     for copy in to_smem:
         copy.wait()
     prepare(0)
+    pl.semaphore_wait(planes_sem, len(along_y))
     post(0)
 
     @pl.when(edge == 1)
@@ -255,14 +260,13 @@
     every = pl.ds(0, SPAN - 1)
     for half in range(2):
         pltpu.make_async_copy(send.at[half, every], send.at[half, every], send_sem.at[half]).wait()
-        pltpu.make_async_copy(arrive.at[half, every], arrive.at[half, every], recv_sem.at[half]).wait()
-
-    def place(j, carry):
-        clip = srcs[j, 0]
-        out[j] = jnp.concatenate([arrive[0, clip], arrive[1, clip]], axis=0)
-        return carry
-
-    lax.fori_loop(0, WSLOT, place, 0)
+        pltpu.make_async_copy(arrive[half].at[every], arrive[half].at[every], recv_sem.at[half]).wait()
+        for part in range(2):
+
+            @pl.when(flip == (half + part) % 2)
+            def _(half=half, part=part):
+                for j in range(WSLOT):
+                    out[j, 2 * part : 2 * part + 2] = arrive[half][srcs[j, 0]]
 
 
 def local(features, clip_lengths, slot_table, gain_one, weight_one, gain_two, weight_two):
@@ -298,7 +302,8 @@
             pltpu.VMEM((TAPS, 3 * C, C), BF16),
             pltpu.VMEM((2, FRAMES, 2, WIDE), BF16),
             pltpu.VMEM((2, SPAN, 2, WIDE), BF16),
-            pltpu.VMEM((2, SPAN, 2, WIDE), BF16),
+            pltpu.VMEM((SPAN, 2, WIDE), BF16),
+            pltpu.VMEM((SPAN, 2, WIDE), BF16),
             pltpu.VMEM((8, 128), jnp.int32),
             pltpu.VMEM((WSLOT, 128), jnp.int32),
             pltpu.SMEM((8, 128), jnp.int32),
@@ -310,6 +315,8 @@
             pltpu.SemaphoreType.DMA((2,)),
             pltpu.SemaphoreType.DMA((2,)),
             pltpu.SemaphoreType.DMA((2,)),
+            pltpu.SemaphoreType.REGULAR,
+            pltpu.SemaphoreType.REGULAR,
         ],
         compiler_params=pltpu.CompilerParams(
             collective_id=0, has_side_effects=True, vmem_limit_bytes=48 * 1024 * 1024

time: 31 us -> 30.3 us (0.977)
  Pallas kernels: 29.8 us -> 29.4 us
    pallas_call x1, Pallas kernels: 29.8 us -> 29.4 us  [local(): pl.pallas_call(kernel, out_shape=pltpu.VMEM((WSLOT, ROWS, WIDE), BF16), i...]
where the time goes in v5:
time: 30.3 us; the launch traced here: 30.1 us
  Pallas kernels  29.4 us (97%)
  local copies, waits for them, and re-layouts  0.68 us (2%)
    pallas_call x1, Pallas kernels, local(): pl.pallas_call(kernel, out_shape=pltpu.VMEM((WSLOT, ROWS, WIDE), BF16), i...  29.4 us
    unnamed x1, local copies, waits for them, and re-layouts  0.68 us

profile of v5, /device:TPU:1, one launch (start us, length us, event | category | flops | bytes accessed | tf_op | source)
XLA Modules:
  0.0 30.1 jit_solution(3760915072637608065)
XLA Ops:
  0.0 29.4 %shard_map.64 = bf16[32,4,768]{2,1,0:T(4,128)(2,1)S(1)} custom-call(bf16[41,4,768]{2,1,0:T(4,128)(2,1)} %bitcast.6, s32[41,64]{1,0:T(8,128)} %bitcast.7, f32[384]{0:T(512)} %gain_one.1, bf16[9,1152,384]{2,1,0:T(8,128)(2,1)} %bitcast.4, f32[384]{0:T(512)} %gain_two.1, bf16[9,1152,384]{2,1,0:T(8,128)(2,1)} %bitcast.5), custom_call_target="tpu_custom_call" | custom-call | tf_op jit(solution)/shard_map/pallas_call | solution.py:284
  29.4 0.7 %copy.8 = bf16[32,4,768]{2,1,0:T(4,128)(2,1)} copy(bf16[32,4,768]{2,1,0:T(4,128)(2,1)S(1)} %shard_map.64) | data formatting | bytes 393216

commit v6 on v5

--- a/solution.py
+++ b/solution.py
@@ -19,11 +19,8 @@
 TAPS = 9
 ACROSS = 4
 DEPTH = 8
-ORDER = [
-    (dy, dx, dz)
-    for dy, dx in ((1, 2), (0, 2), (1, 1), (1, 3), (0, 1), (0, 3), (1, 0), (0, 0))
-    for dz in (4, 3, 5, 2, 6, 1, 7, 0)
-][: SPAN - 1]
+XY = ((1, 2), (0, 2), (1, 1), (1, 3), (0, 1), (0, 3), (1, 0), (0, 0))
+ORDER = [(dy, dx, dz) for dy, dx in XY for dz in (4, 3, 5, 2, 6, 1, 7)] + [(dy, dx, 0) for dy, dx in XY[:-1]]
 LANES = 128
 GROUPS = WIDE // LANES
 F32 = jnp.float32
@@ -114,7 +111,8 @@
         pl.semaphore_signal(barrier, inc=1, device_id={"span": pos, "tile": other}, device_id_type=MESH)
     for other in along_z + along_x + along_y:
         pl.semaphore_signal(barrier, inc=1, device_id={"span": other, "tile": tile}, device_id_type=MESH)
-    for copy in weights[:TAPS] + inputs[2:] + weights[TAPS:]:
+    ahead, after = weights[2:TAPS:3] + weights[0:TAPS:3], weights[1:TAPS:3]
+    for copy in ahead + after + inputs[2:]:
         copy.start()
 
     inputs[0].wait()
@@ -203,9 +201,14 @@
                 device_id={"span": dest, "tile": tile}, device_id_type=MESH,
             ).start()
 
-    for copy in weights[:TAPS]:
+    for copy in weights[TAPS:]:
+        copy.start()
+    for copy in ahead:
         copy.wait()
     product(sh1, taps((2,), 0), 4, v1, total, 0)
+    product(sh1, taps((0,), 4), 2, v1, total, 4)
+    for copy in after:
+        copy.wait()
     pl.semaphore_wait(lines_sem, len(along_x))
     for other in along_y:
         pl.semaphore_signal(planes_sem, inc=1, device_id={"span": other, "tile": tile}, device_id_type=MESH)
@@ -244,9 +247,9 @@
         for row in range(2):
             put_shifts(sh1, 7 - row, far[row].astype(F32))
 
-    product(sh1, taps((0, 1, 2), 4), 2, v1, total, 0)
-    hidden_row(4, 0)
-    hidden_row(5, 1)
+    product(sh1, taps((1, 2), 4), 2, v1, total, 4, add=True)
+    hidden_row(4, 4)
+    hidden_row(5, 5)
     product(sh2, taps((0, 1, 2), 2), 2, v2, total, 0)
     prepare(1)
     post(1)
@@ -297,7 +300,7 @@
             pltpu.VMEM((3, 6, PAD, WIDE), BF16),
             pltpu.VMEM((2, PAD, WIDE), BF16),
             pltpu.VMEM((2, PAD, WIDE), BF16),
-            pltpu.VMEM((4 * PAD, WIDE), F32),
+            pltpu.VMEM((6 * PAD, WIDE), F32),
             pltpu.VMEM((TAPS, 3 * C, C), BF16),
             pltpu.VMEM((TAPS, 3 * C, C), BF16),
             pltpu.VMEM((2, FRAMES, 2, WIDE), BF16),

time: 30.3 us -> 28.7 us (0.947)
  Pallas kernels: 29.4 us -> 28 us
    pallas_call x1, Pallas kernels: 29.4 us -> 28 us  [local(): pl.pallas_call(kernel, out_shape=pltpu.VMEM((WSLOT, ROWS, WIDE), BF16), i...]
where the time goes in v6:
time: 28.7 us
  Pallas kernels  28 us (98%)
  local copies, waits for them, and re-layouts  0.68 us (2%)
    pallas_call x1, Pallas kernels, local(): pl.pallas_call(kernel, out_shape=pltpu.VMEM((WSLOT, ROWS, WIDE), BF16), i...  28 us
    unnamed x1, local copies, waits for them, and re-layouts  0.68 us

profile of v6, /device:TPU:1, one launch (start us, length us, event | category | flops | bytes accessed | tf_op | source)
XLA Modules:
  0.0 28.7 jit_solution(11238300899319023412)
XLA Ops:
  0.0 28.0 %shard_map.64 = bf16[32,4,768]{2,1,0:T(4,128)(2,1)S(1)} custom-call(bf16[41,4,768]{2,1,0:T(4,128)(2,1)} %bitcast.6, s32[41,64]{1,0:T(8,128)} %bitcast.7, f32[384]{0:T(512)} %gain_one.1, bf16[9,1152,384]{2,1,0:T(8,128)(2,1)} %bitcast.4, f32[384]{0:T(512)} %gain_two.1, bf16[9,1152,384]{2,1,0:T(8,128)(2,1)} %bitcast.5), custom_call_target="tpu_custom_call" | custom-call | tf_op jit(solution)/shard_map/pallas_call | solution.py:287
  28.0 0.7 %copy.8 = bf16[32,4,768]{2,1,0:T(4,128)(2,1)} copy(bf16[32,4,768]{2,1,0:T(4,128)(2,1)S(1)} %shard_map.64) | data formatting | bytes 393216

commit v7 on v6

--- a/solution.py
+++ b/solution.py
@@ -121,7 +121,7 @@
         values = raw[f].astype(F32)
         for g in range(GROUPS):
             nat[g, ROWS * f : ROWS * (f + 1), :] = values[:, g * LANES : (g + 1) * LANES]
-    nat[:, ROWS * FRAMES :, :] = jnp.zeros((GROUPS, ROWS * (PAD - FRAMES), LANES), F32)
+    nat[:, ROWS * FRAMES : ROWS * PAD, :] = jnp.zeros((GROUPS, ROWS * (PAD - FRAMES), LANES), F32)
 
     def own_row(step):
         row = lax.rem(step + 2 * edge, ROWS)
@@ -150,8 +150,39 @@
     def _():
         to_far.start()
 
-    inputs[2].wait()
-    inputs[3].wait()
+
+    def hidden_row(row, start):
+        values = activate(total[start * PAD : (start + 1) * PAD, :].astype(BF16).astype(F32), g2[...].reshape(1, C))
+        if row == 0:
+            values = jnp.where(edge == 1, 0.0, values)
+        put_shifts(sh2, row, values)
+
+    def prepare(half):
+        for i in range(2):
+            row = physical(2 * half + i)
+            for g in range(GROUPS):
+                mix[g, pl.ds(lax.rem(row, 2), PAD, stride=2), :] = (
+                    nat[g, pl.ds(row, PAD, stride=ROWS), :]
+                    + total[i * PAD : (i + 1) * PAD, g * LANES : (g + 1) * LANES]
+                )
+        for f in range(FRAMES):
+            block[half, f] = jnp.concatenate([mix[g, 2 * f : 2 * f + 2, :] for g in range(GROUPS)], axis=1).astype(BF16)
+        arrive[half][pos] = block[half, picks[0, pos]]
+
+    def post(half):
+        for dy, dx, dz in ORDER:
+            dest = shifted_by(dy, dx, dz)
+            send[half, dest] = block[half, picks[0, dest]]
+            pltpu.make_async_remote_copy(
+                src_ref=send.at[half, dest], dst_ref=arrive[half].at[pos],
+                send_sem=send_sem.at[half], recv_sem=recv_sem.at[half],
+                device_id={"span": dest, "tile": tile}, device_id_type=MESH,
+            ).start()
+
+    for copy in weights[TAPS:]:
+        copy.start()
+    for copy in inputs[2:] + ahead:
+        copy.wait()
     table = slotv[...]
     lane = lax.broadcasted_iota(jnp.int32, (FRAMES, SPAN), 1)
     column = jnp.sum(jnp.where(lane == pos, table, 0), axis=1, keepdims=True)
@@ -166,47 +197,14 @@
     for f in range(FRAMES):
         found = jnp.where(table[f : f + 1, :] == wanted, clip, found)
     srcv[...] = jnp.broadcast_to(jnp.max(found, axis=1, keepdims=True), (WSLOT, 128))
+    product(sh1, taps((2,), 0), 4, v1, total, 0)
+    product(sh1, taps((0,), 4), 2, v1, total, 4)
     to_smem = [
         pltpu.make_async_copy(pickv, picks, smem_sem.at[0]),
         pltpu.make_async_copy(srcv, srcs, smem_sem.at[1]),
     ]
     for copy in to_smem:
         copy.start()
-
-    def hidden_row(row, start):
-        values = activate(total[start * PAD : (start + 1) * PAD, :].astype(BF16).astype(F32), g2[...].reshape(1, C))
-        if row == 0:
-            values = jnp.where(edge == 1, 0.0, values)
-        put_shifts(sh2, row, values)
-
-    def prepare(half):
-        for i in range(2):
-            row = physical(2 * half + i)
-            for g in range(GROUPS):
-                mix[g, pl.ds(lax.rem(row, 2), PAD, stride=2), :] = (
-                    nat[g, pl.ds(row, PAD, stride=ROWS), :]
-                    + total[i * PAD : (i + 1) * PAD, g * LANES : (g + 1) * LANES]
-                )
-        for f in range(FRAMES):
-            block[half, f] = jnp.concatenate([mix[g, 2 * f : 2 * f + 2, :] for g in range(GROUPS)], axis=1).astype(BF16)
-        arrive[half][pos] = block[half, picks[0, pos]]
-
-    def post(half):
-        for dy, dx, dz in ORDER:
-            dest = shifted_by(dy, dx, dz)
-            send[half, dest] = block[half, picks[0, dest]]
-            pltpu.make_async_remote_copy(
-                src_ref=send.at[half, dest], dst_ref=arrive[half].at[pos],
-                send_sem=send_sem.at[half], recv_sem=recv_sem.at[half],
-                device_id={"span": dest, "tile": tile}, device_id_type=MESH,
-            ).start()
-
-    for copy in weights[TAPS:]:
-        copy.start()
-    for copy in ahead:
-        copy.wait()
-    product(sh1, taps((2,), 0), 4, v1, total, 0)
-    product(sh1, taps((0,), 4), 2, v1, total, 4)
     for copy in after:
         copy.wait()
     pl.semaphore_wait(lines_sem, len(along_x))
@@ -294,8 +292,8 @@
             pltpu.VMEM((FRAMES, SPAN), jnp.int32),
             pltpu.VMEM((C,), F32),
             pltpu.VMEM((C,), F32),
-            pltpu.VMEM((GROUPS, ROWS * PAD, LANES), F32),
-            pltpu.VMEM((GROUPS, 2 * PAD, LANES), F32),
+            pltpu.VMEM((GROUPS, ROWS * PAD + 8, LANES), F32),
+            pltpu.VMEM((GROUPS, 2 * PAD + 8, LANES), F32),
             pltpu.VMEM((3, 8, PAD, WIDE), BF16),
             pltpu.VMEM((3, 6, PAD, WIDE), BF16),
             pltpu.VMEM((2, PAD, WIDE), BF16),

time: 28.7 us -> 28.5 us (level)
  no operation moved by 1% of the time
where the time goes in v7:
time: 28.5 us
  Pallas kernels  27.8 us (98%)
  local copies, waits for them, and re-layouts  0.68 us (2%)
    pallas_call x1, Pallas kernels, local(): pl.pallas_call(kernel, out_shape=pltpu.VMEM((WSLOT, ROWS, WIDE), BF16), i...  27.8 us
    unnamed x1, local copies, waits for them, and re-layouts  0.68 us

profile of v7, /device:TPU:1, one launch (start us, length us, event | category | flops | bytes accessed | tf_op | source)
XLA Modules:
  0.0 28.5 jit_solution(12446403704075478437)
XLA Ops:
  0.0 27.8 %shard_map.64 = bf16[32,4,768]{2,1,0:T(4,128)(2,1)S(1)} custom-call(bf16[41,4,768]{2,1,0:T(4,128)(2,1)} %bitcast.6, s32[41,64]{1,0:T(8,128)} %bitcast.7, f32[384]{0:T(512)} %gain_one.1, bf16[9,1152,384]{2,1,0:T(8,128)(2,1)} %bitcast.4, f32[384]{0:T(512)} %gain_two.1, bf16[9,1152,384]{2,1,0:T(8,128)(2,1)} %bitcast.5), custom_call_target="tpu_custom_call" | custom-call | tf_op jit(solution)/shard_map/pallas_call | solution.py:285
  27.8 0.7 %copy.8 = bf16[32,4,768]{2,1,0:T(4,128)(2,1)} copy(bf16[32,4,768]{2,1,0:T(4,128)(2,1)S(1)} %shard_map.64) | data formatting | bytes 393216
